TPU v7x, 32 devices: a whole 2x2x4 slice. The times are simulated.
32 devices in a mesh: cells: 8 (over y, x, core), stations: 4 (over z).
Axes of the slice: x: 2, y: 2, z: 4, core: 2. Of those that a mesh axis runs over, the one named last changes fastest.
Arguments:
- probes: bfloat16 [16, 32768], P(None, 'cells'), may hold values from -6 to 6
- reg_weight: float32 [32768], P('cells'), may hold values from 0.1 to 1
- cell_plan: int32 [2, 32768], P(None, 'cells'), may hold values from 0 to 255
- cell_depth: int32 [32768], P('cells'), may hold values from 0 to 15, as said below
- station_index: int32 [2, 16384], P(None, 'stations'), may hold values from 0 to 65535, as said below
- station_weight: float32 [16384], P('stations'), may hold values from 0.5 to 2
Outputs:
- basis: float32 [16, 32768], P(None, ('cells', 'stations'))
- factor: float32 [16, 16], replicated
Inputs may be any that keep to these rules, and one draw needn't show every extreme that they name: `cell_plan`: east and north cell indices of a grid of 256 by 256 columns. `cell_depth`: depth indices of 16 layers. `station_index`: east and north station positions in 1/256ths of a cell width, over the same area as the cells' grid.
All inputs are finite; a program needn't handle non-finite values.
Results may differ from a plain program's by a relative error of at most 0.00065.
Values may be sent and summed in bfloat16 or wider, within the bound.
A program may use at most 64 MiB of HBM per device.

v0:
```python
import functools
import math

import jax
import jax.numpy as jnp
from jax import lax
from jax.experimental import pallas as pl
from jax.experimental.pallas import tpu as pltpu
from jax.sharding import PartitionSpec as P

JITTER = 1e-06
MESH = pl.DeviceIdType.MESH
F32 = jnp.float32
BF16 = jnp.bfloat16
TILE = 256
FEATURES = 16


def matmul(left, right):
    return jnp.dot(left, right, preferred_element_type=F32)


def matmul_nt(left, right, precision=None):
    return lax.dot_general(
        left, right, (((1,), (1,)), ((), ())), precision=precision, preferred_element_type=F32
    )


def cell_features(plan_ref, depth_ref):
    east = plan_ref[0:1, :] - 128
    north = plan_ref[1:2, :] - 128
    down = depth_ref[...] + 1
    square = east * east + north * north + down * down
    high = (square >> 8) << 8
    low = square & 255
    one = jnp.ones_like(square)
    zero = jnp.zeros_like(square)
    rows = [high, low, one, one, east, north, zero, zero]
    rows += [east, north, one, one, one, zero, zero, zero]
    return jnp.concatenate([row.astype(F32) for row in rows], axis=0)


def station_features(index_ref):
    east, north = index_ref[0:1, :], index_ref[1:2, :]
    whole_e, whole_n = (east >> 8) - 128, (north >> 8) - 128
    part_e, part_n = (east & 255) - 128, (north & 255) - 128
    square = whole_e * whole_e + whole_n * whole_n
    cross = 512 * (whole_e * part_e + whole_n * part_n) + part_e * part_e + part_n * part_n
    one = jnp.ones_like(square).astype(F32)
    zero = jnp.zeros_like(one)
    rows = [
        one,
        one,
        ((square >> 8) << 8).astype(F32),
        (square & 255).astype(F32),
        (-2 * whole_e).astype(F32),
        (-2 * whole_n).astype(F32),
        zero,
        zero,
        part_e.astype(F32) * (-2.0 / 256),
        part_n.astype(F32) * (-2.0 / 256),
        (cross >> 16).astype(F32),
        ((cross >> 8) & 255).astype(F32) * (1.0 / 256),
        (cross & 255).astype(F32) * (1.0 / 65536),
        zero,
        zero,
        zero,
    ]
    return jnp.concatenate(rows, axis=0)


def kernel(
    n_cells,
    n_stations,
    probes_ref,
    reg_ref,
    plan_ref,
    depth_ref,
    index_ref,
    weight_ref,
    basis_ref,
    factor_ref,
    sens,
    cell_feat,
    station_feat,
    scale,
    running,
    field_out,
    field_in,
    weighted,
    image_out,
    image_in,
    gram_s,
    gram_c,
    field_send,
    field_recv,
    weighted_send,
    weighted_recv,
    image_send,
    image_recv,
    gs_send,
    gs_recv,
    gc_send,
    gc_recv,
):
    k_rows, cells = probes_ref.shape
    stations = index_ref.shape[1]
    own = stations // n_cells
    quarter = cells // n_stations
    block = max(own, 512)
    block_owners = block // own
    blocks = stations // block
    me_c = lax.axis_index("cells")
    me_s = lax.axis_index("stations")

    def peer_c(step):
        return lax.rem(me_c + step, n_cells)

    def peer_s(step):
        return lax.rem(me_s + step, n_stations)

    barrier = pltpu.get_barrier_semaphore()

    def greet_c(step, carry):
        pl.semaphore_signal(barrier, inc=1, device_id={"cells": peer_c(step)}, device_id_type=MESH)
        return carry

    lax.fori_loop(1, n_cells, greet_c, 0)
    for step in range(1, n_stations):
        pl.semaphore_signal(
            barrier, inc=1, device_id={"stations": peer_s(step)}, device_id_type=MESH
        )

    def field_copy(dest):
        return pltpu.make_async_remote_copy(
            src_ref=field_out.at[dest],
            dst_ref=field_in.at[me_c],
            send_sem=field_send.at[dest],
            recv_sem=field_recv.at[me_c],
            device_id={"cells": dest},
            device_id_type=MESH,
        )

    def field_arrival(source):
        return pltpu.make_async_remote_copy(
            src_ref=field_out.at[source],
            dst_ref=field_in.at[source],
            send_sem=field_send.at[source],
            recv_sem=field_recv.at[source],
            device_id={"cells": source},
            device_id_type=MESH,
        )

    def weighted_copy(dest, source):
        return pltpu.make_async_remote_copy(
            src_ref=weighted.at[source],
            dst_ref=weighted.at[source],
            send_sem=weighted_send.at[dest],
            recv_sem=weighted_recv.at[source],
            device_id={"cells": dest},
            device_id_type=MESH,
        )

    def image_copy(dest, source):
        return pltpu.make_async_remote_copy(
            src_ref=image_out.at[dest],
            dst_ref=image_in.at[source],
            send_sem=image_send.at[dest],
            recv_sem=image_recv.at[source],
            device_id={"stations": dest},
            device_id_type=MESH,
        )

    def gs_copy(dest, source):
        return pltpu.make_async_remote_copy(
            src_ref=gram_s.at[source],
            dst_ref=gram_s.at[source],
            send_sem=gs_send.at[dest],
            recv_sem=gs_recv.at[source],
            device_id={"stations": dest},
            device_id_type=MESH,
        )

    def gc_copy(dest, source):
        return pltpu.make_async_remote_copy(
            src_ref=gram_c.at[source],
            dst_ref=gram_c.at[source],
            send_sem=gc_send.at[dest],
            recv_sem=gc_recv.at[source],
            device_id={"cells": dest},
            device_id_type=MESH,
        )

    cell_feat[...] = cell_features(plan_ref, depth_ref).astype(BF16)
    scale[...] = (depth_ref[...].astype(F32) + 1.0) * 2.0
    features = station_features(index_ref)
    padded = jnp.concatenate(
        [features, jnp.zeros((128 - FEATURES, stations), F32)], axis=0
    )
    station_feat[...] = padded.T[:, :FEATURES].astype(BF16)

    own_block = me_c // block_owners
    width = math.gcd(cells, 8 * TILE)
    chunks = cells // width
    pieces = block // TILE

    def place(turn):
        index = lax.rem(own_block + 1 + turn // chunks, blocks)
        return index, pl.multiple_of(index * block, block), lax.rem(turn, chunks)

    def make_tiles(turn):
        _, start, chunk = place(turn)
        for step in range(width // TILE):
            columns = pl.ds(pl.multiple_of(chunk * width + step * TILE, TILE), TILE)
            factor2 = scale[:, columns]
            rows = pl.ds(start, block)
            distance = matmul(station_feat[rows, :], cell_feat[:, columns])
            inverse = lax.rsqrt(distance)
            sens[rows, columns] = (factor2 * inverse * inverse * inverse).astype(BF16)

    def use_tiles(turn):
        _, start, chunk = place(turn)
        columns = pl.ds(pl.multiple_of(chunk * width, width), width)
        vectors = probes_ref[:, columns]
        for piece in range(pieces):
            rows = pl.ds(start + piece * TILE, TILE)
            into = pl.ds(piece * TILE, TILE)
            before = jnp.where(chunk == 0, 0.0, running[:, into])
            running[:, into] = before + matmul_nt(vectors, sens[rows, columns])

    def send_field(turn):
        index, start, chunk = place(turn)

        @pl.when(chunk == chunks - 1)
        def _():
            station_scale = weight_ref[:, pl.ds(start, block)]
            field = running[...] * (station_scale * station_scale)
            for part in range(block_owners):
                dest = index * block_owners + part
                field_out[dest] = field[:, part * own : (part + 1) * own]

                @pl.when(dest != me_c)
                def _():
                    field_copy(dest).start()

    running[...] = jnp.zeros_like(running)
    make_tiles(0)
    pl.semaphore_wait(barrier, n_cells - 1 + n_stations - 1)

    def forward(turn, carry):
        use_tiles(turn - 1)
        make_tiles(turn)
        send_field(turn - 1)
        return carry

    lax.fori_loop(1, blocks * chunks, forward, 0)
    use_tiles(blocks * chunks - 1)
    send_field(blocks * chunks - 1)

    def add_field(step, before):
        source = peer_c(step)
        field_arrival(source).wait_recv()
        return before + field_in[source]

    total = lax.fori_loop(1, n_cells, add_field, field_out[me_c])
    weighted[me_c] = total.astype(BF16)

    def send_weighted(step, carry):
        weighted_copy(peer_c(step), me_c).start()
        return carry

    lax.fori_loop(1, n_cells, send_weighted, 0)

    def await_weighted(step, carry):
        weighted_copy(peer_c(step), peer_c(step)).wait_recv()
        return carry

    lax.fori_loop(1, n_cells, await_weighted, 0)

    offsets = [2, 1, 3, 0] if n_stations == 4 else list(range(n_stations - 1, -1, -1))
    image = None
    for offset in offsets:
        dest = peer_s(offset)
        columns = pl.ds(pl.multiple_of(dest * quarter, quarter), quarter)

        def backward(step, before):
            rows = pl.ds(pl.multiple_of(step * own, own), own)
            return before + matmul(weighted[step], sens[rows, columns])

        partial = lax.fori_loop(0, n_cells, backward, jnp.zeros((k_rows, quarter), F32), unroll=4)
        if offset:
            image_out[dest] = partial
            image_copy(dest, me_s).start()
        else:
            image = partial + reg_ref[:, columns] * probes_ref[:, columns].astype(F32)

    for step in range(1, n_stations):
        source = peer_s(step)
        image_copy(source, source).wait_recv()
        image = image + image_in[source]

    gram = matmul_nt(image, image, lax.Precision.HIGHEST)
    gram_s[me_s] = gram
    for step in range(1, n_stations):
        gs_copy(peer_s(step), me_s).start()
    for step in range(1, n_stations):
        gs_copy(peer_s(step), peer_s(step)).wait_recv()
    gram = gram_s[0]
    for source in range(1, n_stations):
        gram = gram + gram_s[source]
    gram_c[me_c] = gram

    def send_gram(step, carry):
        gc_copy(peer_c(step), me_c).start()
        return carry

    def await_gram(step, carry):
        gc_copy(peer_c(step), peer_c(step)).wait_recv()
        return carry

    lax.fori_loop(1, n_cells, send_gram, 0)
    lax.fori_loop(1, n_cells, await_gram, 0)
    gram = lax.fori_loop(1, n_cells, lambda s, r: r + gram_c[s], gram_c[0])

    row = lax.broadcasted_iota(jnp.int32, (k_rows, k_rows), 0)
    col = lax.broadcasted_iota(jnp.int32, (k_rows, k_rows), 1)
    left = gram / (cells * n_cells) + jnp.where(row == col, JITTER, 0.0)
    lower = jnp.zeros_like(left)
    row1 = row[:, 0:1]
    for j in range(k_rows):
        pivot = left[j : j + 1, j : j + 1]
        column = left[:, j : j + 1]
        lower = jnp.where((col == j) & (row >= j), column * lax.rsqrt(pivot), lower)
        ratio = jnp.where(row1 > j, column / pivot, 0.0)
        left = left - ratio * left[j : j + 1, :]
        image = image - ratio * image[j : j + 1, :]
    diagonal = jnp.sum(jnp.where(row == col, left, 0.0), axis=1, keepdims=True)
    basis_ref[...] = image * lax.rsqrt(diagonal)
    factor_ref[...] = lower

    def finish_c(step, carry):
        dest = peer_c(step)
        field_copy(dest).wait_send()
        weighted_copy(dest, me_c).wait_send()
        gc_copy(dest, me_c).wait_send()
        return carry

    lax.fori_loop(1, n_cells, finish_c, 0)
    for step in range(1, n_stations):
        dest = peer_s(step)
        image_copy(dest, me_s).wait_send()
        gs_copy(dest, me_s).wait_send()


def body(n_cells, n_stations, probes, reg_weight, cell_plan, cell_depth, station_index, station_weight):
    k_rows, cells = probes.shape
    stations = station_index.shape[1]
    own = stations // n_cells
    quarter = cells // n_stations
    dma = pltpu.SemaphoreType.DMA
    return pl.pallas_call(
        functools.partial(kernel, n_cells, n_stations),
        out_shape=(
            jax.ShapeDtypeStruct((k_rows, quarter), F32),
            jax.ShapeDtypeStruct((k_rows, k_rows), F32),
        ),
        in_specs=[pl.BlockSpec(memory_space=pltpu.VMEM)] * 6,
        out_specs=(pl.BlockSpec(memory_space=pltpu.VMEM),) * 2,
        scratch_shapes=[
            pltpu.VMEM((stations, cells), BF16),
            pltpu.VMEM((FEATURES, cells), BF16),
            pltpu.VMEM((stations, FEATURES), BF16),
            pltpu.VMEM((1, cells), F32),
            pltpu.VMEM((k_rows, max(own, 512)), F32),
            pltpu.VMEM((n_cells, k_rows, own), F32),
            pltpu.VMEM((n_cells, k_rows, own), F32),
            pltpu.VMEM((n_cells, k_rows, own), BF16),
            pltpu.VMEM((n_stations, k_rows, quarter), F32),
            pltpu.VMEM((n_stations, k_rows, quarter), F32),
            pltpu.VMEM((n_stations, k_rows, k_rows), F32),
            pltpu.VMEM((n_cells, k_rows, k_rows), F32),
            dma((n_cells,)),
            dma((n_cells,)),
            dma((n_cells,)),
            dma((n_cells,)),
            dma((n_stations,)),
            dma((n_stations,)),
            dma((n_stations,)),
            dma((n_stations,)),
            dma((n_cells,)),
            dma((n_cells,)),
        ],
        compiler_params=pltpu.CompilerParams(
            collective_id=0, has_side_effects=True, vmem_limit_bytes=56 * 1024 * 1024
        ),
    )(
        probes,
        reg_weight.reshape(1, -1),
        cell_plan,
        cell_depth.reshape(1, -1),
        station_index,
        station_weight.reshape(1, -1),
    )


def solution(mesh):
    return jax.shard_map(
        functools.partial(body, mesh.shape["cells"], mesh.shape["stations"]),
        mesh=mesh,
        in_specs=(
            P(None, "cells"),
            P("cells"),
            P(None, "cells"),
            P("cells"),
            P(None, "stations"),
            P("stations"),
        ),
        out_specs=(P(None, ("cells", "stations")), P()),
        check_vma=False,
    )
```

profile of v0, /device:TPU:0, one launch (start us, length us, event | category | flops | bytes accessed | tf_op | source)
XLA Modules:
  0.0 55.5 jit_solution(11826632570580328194)
XLA Ops:
  0.6 52.7 %shard_map.77 = (f32[16,1024]{1,0:T(8,128)}, f32[16,16]{1,0:T(8,128)}) custom-call(bf16[16,4096]{1,0:T(8,128)(2,1)} %probes_ref.1, f32[1,4096]{1,0:T(1,128)} %bitcast.3, s32[2,4096]{1,0:T(2,128)} %plan_ref.1, s32[1,4096]{1,0:T(1,128)} %bitcast.4, s32[2,4096]{1,0:T(2,128)} %index_ref.1, f32[1,4096]{1,0:T(1,128)} %bitcast.5), custom_call_target="tpu_custom_call" | custom-call | tf_op jit(solution)/shard_map/pallas_call | solution.py:361
  53.4 0.0 copy-start
  53.4 1.5 %copy.10 = f32[16,1024]{1,0:T(8,128)} copy(f32[16,1024]{1,0:T(8,128)} %get-tuple-element.4) | data formatting | bytes 131072
  54.9 0.0 copy-done
  54.9 0.6 %copy.11 = f32[16,16]{1,0:T(8,128)} copy(f32[16,16]{1,0:T(8,128)S(1)} %copy-done) | data formatting | bytes 2048
Async XLA Ops:
  53.4 1.5 %copy-start = (f32[16,16]{1,0:T(8,128)S(1)}, f32[16,16]{1,0:T(8,128)}, u32[]{:S(2)}) copy-start(f32[16,16]{1,0:T(8,128)} %get-tuple-element.5) | copy-start | bytes 3076
where the time goes:
time: 55.7 us; the launch traced here: 55.5 us
  Pallas kernels  52.7 us (95%)
  local copies, waits for them, and re-layouts  2.08 us (4%)
  between operations  0.65 us (1%)
    pallas_call x1, Pallas kernels, body(): pl.pallas_call(functools.partial(kernel, n_cells, n_stations), out_shape=...  52.7 us
    unnamed x4, local copies, waits for them, and re-layouts  2.08 us

commit v1 on v0

--- a/solution.py
+++ b/solution.py
@@ -78,8 +78,8 @@
     depth_ref,
     index_ref,
     weight_ref,
-    basis_ref,
-    factor_ref,
+    image_ref,
+    gram_ref,
     sens,
     cell_feat,
     station_feat,
@@ -194,10 +194,7 @@
     cell_feat[...] = cell_features(plan_ref, depth_ref).astype(BF16)
     scale[...] = (depth_ref[...].astype(F32) + 1.0) * 2.0
     features = station_features(index_ref)
-    padded = jnp.concatenate(
-        [features, jnp.zeros((128 - FEATURES, stations), F32)], axis=0
-    )
-    station_feat[...] = padded.T[:, :FEATURES].astype(BF16)
+    station_feat[...] = features.T.astype(BF16)
 
     own_block = me_c // block_owners
     width = math.gcd(cells, 8 * TILE)
@@ -322,9 +319,29 @@
     lax.fori_loop(1, n_cells, await_gram, 0)
     gram = lax.fori_loop(1, n_cells, lambda s, r: r + gram_c[s], gram_c[0])
 
+    image_ref[...] = image
+    gram_ref[...] = gram / (cells * n_cells)
+
+    def finish_c(step, carry):
+        dest = peer_c(step)
+        field_copy(dest).wait_send()
+        weighted_copy(dest, me_c).wait_send()
+        gc_copy(dest, me_c).wait_send()
+        return carry
+
+    lax.fori_loop(1, n_cells, finish_c, 0)
+    for step in range(1, n_stations):
+        dest = peer_s(step)
+        image_copy(dest, me_s).wait_send()
+        gs_copy(dest, me_s).wait_send()
+
+
+def orthonormalize(image_ref, gram_ref, basis_ref, factor_ref):
+    k_rows = image_ref.shape[0]
+    image = image_ref[...]
     row = lax.broadcasted_iota(jnp.int32, (k_rows, k_rows), 0)
     col = lax.broadcasted_iota(jnp.int32, (k_rows, k_rows), 1)
-    left = gram / (cells * n_cells) + jnp.where(row == col, JITTER, 0.0)
+    left = gram_ref[...] + jnp.where(row == col, JITTER, 0.0)
     lower = jnp.zeros_like(left)
     row1 = row[:, 0:1]
     for j in range(k_rows):
@@ -338,19 +355,6 @@
     basis_ref[...] = image * lax.rsqrt(diagonal)
     factor_ref[...] = lower
 
-    def finish_c(step, carry):
-        dest = peer_c(step)
-        field_copy(dest).wait_send()
-        weighted_copy(dest, me_c).wait_send()
-        gc_copy(dest, me_c).wait_send()
-        return carry
-
-    lax.fori_loop(1, n_cells, finish_c, 0)
-    for step in range(1, n_stations):
-        dest = peer_s(step)
-        image_copy(dest, me_s).wait_send()
-        gs_copy(dest, me_s).wait_send()
-
 
 def body(n_cells, n_stations, probes, reg_weight, cell_plan, cell_depth, station_index, station_weight):
     k_rows, cells = probes.shape
@@ -358,12 +362,13 @@
     own = stations // n_cells
     quarter = cells // n_stations
     dma = pltpu.SemaphoreType.DMA
-    return pl.pallas_call(
+    shapes = (
+        jax.ShapeDtypeStruct((k_rows, quarter), F32),
+        jax.ShapeDtypeStruct((k_rows, k_rows), F32),
+    )
+    image, gram = pl.pallas_call(
         functools.partial(kernel, n_cells, n_stations),
-        out_shape=(
-            jax.ShapeDtypeStruct((k_rows, quarter), F32),
-            jax.ShapeDtypeStruct((k_rows, k_rows), F32),
-        ),
+        out_shape=shapes,
         in_specs=[pl.BlockSpec(memory_space=pltpu.VMEM)] * 6,
         out_specs=(pl.BlockSpec(memory_space=pltpu.VMEM),) * 2,
         scratch_shapes=[
@@ -401,6 +406,7 @@
         station_index,
         station_weight.reshape(1, -1),
     )
+    return pl.pallas_call(orthonormalize, out_shape=shapes)(image, gram)
 
 
 def solution(mesh):

time: 55.7 us -> 55.1 us (0.989)
  local copies, waits for them, and re-layouts: 2.08 us -> 0 us
  Pallas kernels: 52.7 us -> 54.2 us
    pallas_call x0 -> x1, Pallas kernels: none -> 2.77 us  [body(): return pl.pallas_call(orthonormalize, out_shape=shapes)(image, gram)]
    unnamed x4 -> x0, local copies, waits for them, and re-layouts: 2.08 us -> none
    pallas_call x1, Pallas kernels: 52.7 us -> 51.5 us  [body(): pl.pallas_call(functools.partial(kernel, n_cells, n_stations), out_shape=...]
where the time goes in v1:
time: 55.1 us; the launch traced here: 54.9 us
  Pallas kernels  54.2 us (98%)
  between operations  0.64 us (1%)
    pallas_call x1, Pallas kernels, body(): pl.pallas_call(functools.partial(kernel, n_cells, n_stations), out_shape=...  51.5 us
    pallas_call x1, Pallas kernels, body(): return pl.pallas_call(orthonormalize, out_shape=shapes)(image, gram)  2.77 us

profile of v1, /device:TPU:0, one launch (start us, length us, event | category | flops | bytes accessed | tf_op | source)
XLA Modules:
  0.0 54.9 jit_solution(10976497775905386644)
XLA Ops:
  0.6 51.5 %shard_map.77 = (f32[16,1024]{1,0:T(8,128)}, f32[16,16]{1,0:T(8,128)}) custom-call(bf16[16,4096]{1,0:T(8,128)(2,1)} %probes_ref.1, f32[1,4096]{1,0:T(1,128)} %bitcast.3, s32[2,4096]{1,0:T(2,128)} %plan_ref.1, s32[1,4096]{1,0:T(1,128)} %bitcast.4, s32[2,4096]{1,0:T(2,128)} %index_ref.1, f32[1,4096]{1,0:T(1,128)} %bitcast.5), custom_call_target="tpu_custom_call" | custom-call | tf_op jit(solution)/shard_map/pallas_call | solution.py:369
  52.1 2.8 %shard_map.78 = (f32[16,1024]{1,0:T(8,128)}, f32[16,16]{1,0:T(8,128)}) custom-call(f32[16,1024]{1,0:T(8,128)} %get-tuple-element.4.image_ref, f32[16,16]{1,0:T(8,128)} %get-tuple-element.5.gram_ref), custom_call_target="tpu_custom_call" | custom-call | tf_op jit(solution)/shard_map/pallas_call | solution.py:409
